TPU v7x, 512 devices: a whole 4x8x8 slice. The times are simulated.
512 devices in a mesh: tile: 64 (over y_hi, z, core), dir: 8 (over x, y_lo).
Axes of the slice: x: 4, y: 8 (y_hi: 4, y_lo: 2; y = y_hi * 2 + y_lo), z: 8, core: 2. Of those that a mesh axis runs over, the one named last changes fastest.
Arguments:
- coherency: bfloat16 [128, 48, 12, 8, 256], P('tile', 'dir'), may hold values from -0.59765625 to 0.59765625
- observed: bfloat16 [128, 12, 8, 256], P('tile'), may hold values from -12 to 12
- flags: int32 [128, 3], P('tile'), may hold values 0 or 1
- tile_map: int32 [128, 2], P('tile'), may hold values from 0 to 31, as said below
- jones: float32 [48, 8, 512], P('dir', None, 'tile'), may hold values from -6 to 6
Outputs:
- residual: float32 [128, 12, 8, 256], P('tile', None, None, 'dir')
- gradient: float32 [48, 8, 512], P('dir', None, 'tile')
- curvature: float32 [48, 2, 512], P('dir', None, 'tile')
Inputs may be any that keep to these rules, and one draw needn't show every extreme that they name: `tile_map`: each row names a station block pair (row block, column block) with row block <= column block; no pair appears twice.
All inputs are finite; a program needn't handle non-finite values. No bound on the sum of `flags` on one device may be relied on, other than what follows from the above.
Results may differ from a plain program's by a relative error of at most 0.00035.
Values sent between devices are 32-bit elements; how exact they have to be, the bound alone decides.
A program may use at most 64 MiB of HBM per device.

v0:
```python
import jax
import jax.numpy as jnp
from jax import lax
from jax.sharding import PartitionSpec as P

SB = 16
FREQ_CHANNELS = 4


def split_parts(values):
    shape = values.shape[:-2] + (2, 2, values.shape[-1])
    return (values[..., 0:4, :].reshape(shape), values[..., 4:8, :].reshape(shape))


def join_parts(re_part, im_part):
    shape = re_part.shape[:-3] + (4, re_part.shape[-1])
    return jnp.concatenate([re_part.reshape(shape), im_part.reshape(shape)], axis=-2)


def complex_product(left_re, left_im, right_re, right_im):
    lre = left_re[..., :, :, None, :]
    lim = left_im[..., :, :, None, :]
    rre = right_re[..., None, :, :, :]
    rim = right_im[..., None, :, :, :]
    return (jnp.sum(lre * rre - lim * rim, axis=-3), jnp.sum(lre * rim + lim * rre, axis=-3))


def adjoint(re_part, im_part):
    return (jnp.swapaxes(re_part, -3, -2), -jnp.swapaxes(im_part, -3, -2))


def weights(row_flag_mask, block_pair):
    valid_samples = jnp.repeat((1 - row_flag_mask).astype(jnp.float32), FREQ_CHANNELS)
    baseline = jnp.arange(SB * SB, dtype=jnp.int32)
    inner_row = baseline // SB
    inner_col = baseline % SB
    upper_triangle_pairs = jnp.where(
        (block_pair[0] < block_pair[1]) | (inner_row < inner_col), 1.0, 0.0
    ).astype(jnp.float32)
    return valid_samples[:, None, None] * upper_triangle_pairs[None, None, :]


def tile_terms(coher, jones_all, block_pair):
    row_gain_matrix = lax.dynamic_slice_in_dim(jones_all, block_pair[0] * SB, SB, 2)
    col_jones = lax.dynamic_slice_in_dim(jones_all, block_pair[1] * SB, SB, 2)
    first_antenna = jnp.repeat(row_gain_matrix, SB, axis=2)[:, None]
    station_q = jnp.tile(col_jones, (1, 1, SB))[:, None]
    coh_re, coh_im = split_parts(coher)
    p_re, p_im = split_parts(first_antenna)
    q_re, q_im = split_parts(station_q)
    qh_re, qh_im = adjoint(q_re, q_im)
    m_re, m_im = complex_product(coh_re, coh_im, qh_re, qh_im)
    n_re, n_im = complex_product(p_re, p_im, coh_re, coh_im)
    v_re, v_im = complex_product(p_re, p_im, m_re, m_im)
    predicted = jnp.sum(join_parts(v_re, v_im), axis=0)
    return (predicted, (m_re, m_im, n_re, n_im))


def station_terms(residual, weight, products):
    m_re, m_im, n_re, n_im = products
    r_re, r_im = split_parts(residual)
    mh_re, mh_im = adjoint(m_re, m_im)
    g_re, g_im = complex_product(r_re, r_im, mh_re, mh_im)
    row_side = jnp.sum(join_parts(g_re, g_im), axis=1)
    rh_re, rh_im = adjoint(r_re, r_im)
    f_re, f_im = complex_product(rh_re, rh_im, n_re, n_im)
    col_side = jnp.sum(join_parts(f_re, f_im), axis=1)
    row_curv = jnp.sum(jnp.sum(m_re * m_re + m_im * m_im, axis=-2) * weight[None], axis=1)
    column_curvature = jnp.sum(jnp.sum(n_re * n_re + n_im * n_im, axis=-3) * weight[None], axis=1)
    lead = row_side.shape[0]
    grad_row = jnp.sum(row_side.reshape(lead, 8, SB, SB), axis=3)
    grad_col = jnp.sum(col_side.reshape(lead, 8, SB, SB), axis=2)
    curv_row = jnp.sum(row_curv.reshape(lead, 2, SB, SB), axis=3)
    curv_col = jnp.sum(column_curvature.reshape(lead, 2, SB, SB), axis=2)
    return (grad_row, grad_col, curv_row, curv_col)


def add_block(total, piece, block):
    offset = block * SB
    current = lax.dynamic_slice_in_dim(total, offset, SB, 2)
    return lax.dynamic_update_slice_in_dim(total, current + piece, offset, 2)


def body(coherency, observed, flags, tile_map, jones):
    jones_all = lax.all_gather(jones, "tile", axis=2, tiled=True)
    how_many = coherency.shape[0]
    predictions = []
    products_list = []
    weight_list = []
    for number in range(how_many):
        predicted, products = tile_terms(
            coherency[number].astype(jnp.float32), jones_all, tile_map[number]
        )
        predictions.append(predicted)
        products_list.append(products)
        weight_list.append(weights(flags[number], tile_map[number]))
    partial_value = jnp.stack(predictions)
    weight = jnp.stack(weight_list)
    columns = observed.shape[3]
    portion = columns // lax.axis_size("dir")
    offset = lax.axis_index("dir") * portion
    summed = lax.psum(partial_value, "dir")
    residual = weight * (observed.astype(jnp.float32) - summed)
    residual_mine = lax.dynamic_slice_in_dim(residual, offset, portion, 3)
    grad_total = jnp.zeros((jones_all.shape[0], 8, jones_all.shape[2]), jnp.float32)
    curv_total = jnp.zeros((jones_all.shape[0], 2, jones_all.shape[2]), jnp.float32)
    for number in range(how_many):
        grad_row, grad_col, curv_row, curv_col = station_terms(
            residual[number], weight[number], products_list[number]
        )
        block_pair = tile_map[number]
        grad_total = add_block(
            add_block(grad_total, grad_row, block_pair[0]), grad_col, block_pair[1]
        )
        curv_total = add_block(
            add_block(curv_total, curv_row, block_pair[0]), curv_col, block_pair[1]
        )
    grad_owned, curv_owned = (
        lax.psum_scatter(grad_total, "tile", scatter_dimension=2, tiled=True),
        lax.psum_scatter(curv_total, "tile", scatter_dimension=2, tiled=True),
    )
    normalizer = 1.0 / (observed.shape[1] * SB)
    return (residual_mine, grad_owned * normalizer, curv_owned * normalizer)


def solution(mesh):
    return jax.shard_map(
        body,
        mesh=mesh,
        in_specs=(
            P("tile", "dir", None, None, None),
            P("tile", None, None, None),
            P("tile", None),
            P("tile", None),
            P("dir", None, "tile"),
        ),
        out_specs=(P("tile", None, None, "dir"), P("dir", None, "tile"), P("dir", None, "tile")),
        check_vma=False,
    )
```

profile of v0, /device:TPU:1, one launch (start us, length us, event | category | flops | bytes accessed | tf_op | source)
XLA Modules:
  0.0 917.5 jit_solution(12687598251085437046)
XLA Ops:
  7.2 1.5 fusion.9
  11.2 1.2 bitcast_convert_fusion.1
  12.4 0.3 fusion.3
  12.6 0.2 mul.682
  12.9 0.2 mul.336
  13.2 97.3 %all_gather.3 = f32[6,8,512]{1,0,2:T(8,128)S(1)} all-gather(f32[6,8,8]{1,0,2:T(8,128)S(1)} %copy.45), channel_id=1, replica_groups=mesh['tile'=64,'dir'=8] {'tile'}, dimensions={2}, use_global_device_ids=true | all-gather | bytes 99840 | tf_op jit(solution)/shard_map/all_gather | solution.py:85
  110.5 0.7 constant_dynamic-slice_fusion.3
  111.2 0.2 broadcast_in_dim.27
  111.4 0.2 broadcast_in_dim_reshape.5
  111.8 0.2 tile.19
  112.0 2.9 subtract_reduce_fusion.1
  115.0 1.1 subtract_reduce_fusion.6
  116.1 1.0 reshape.322
  117.1 1.0 reshape.321
  118.0 0.2 mul.317
  118.3 0.2 mul.310
  118.6 0.2 broadcast_in_dim.26
  118.8 0.2 broadcast_in_dim_reshape.4
  119.0 0.6 mul.324
  119.6 0.6 mul.308
  120.4 0.2 tile.17
  120.7 3.6 subtract_reduce_fusion.4
  124.3 1.9 subtract_reduce_fusion.8
  126.2 1.2 reshape.319
  127.4 1.0 reshape.318
  128.5 1.1 maximum_reduce_fusion
  129.6 0.7 pad_maximum_fusion
  130.3 0.2 all-reduce.7.cloned.1.call-start
  133.0 0.6 add_reduce_fusion.13
  133.6 0.6 add_reduce_fusion.11
  134.8 0.2 copy.55
  135.0 0.2 copy.54
  135.5 0.2 add_reduce_fusion.12
  136.2 1.0 dynamic_update_slice.28
  137.3 0.2 dynamic_update_slice.29
  137.5 0.2 add_reduce_fusion.10
  138.2 1.0 dynamic_update_slice.30
  139.4 1.0 dynamic_update_slice.31
  140.4 268.9 %all-reduce.1 = f32[6,2,512]{2,1,0:T(2,128)S(1)} all-reduce(f32[6,2,512]{2,1,0:T(2,128)S(1)} %dynamic_update_slice.31), channel_id=3, replica_groups=mesh['tile'=64,'dir'=8] {'tile'}, use_global_device_ids=true, to_apply=%region_44.45.clone | all-reduce | flops 6144 | bytes 49152
  409.3 1.3 dynamic-slice
  411.2 0.7 dynamic-slice_multiply_fusion.1
  411.9 1.0 subtract_multiply_fusion
  413.0 1.1 subtract_reduce_fusion.5
  414.2 0.3 reshape.324
  414.4 0.3 reshape.323
  415.0 0.2 reduce_sum.391
  415.2 1.1 subtract_reduce_fusion.3
  416.4 0.3 reshape.327
  416.7 0.3 reshape.326
  417.3 1.1 dynamic_update_slice.24
  418.4 0.3 dynamic_update_slice.25
  418.9 1.1 subtract_reduce_fusion.2
  420.0 0.3 reshape.330
  420.3 0.3 reshape.329
  420.9 0.2 reduce_sum.401
  421.1 1.0 dynamic_update_slice.26
  422.2 1.1 subtract_reduce_fusion
  423.4 0.3 reshape.333
  423.6 0.3 reshape.332
  424.3 1.0 dynamic_update_slice.27
  425.3 0.6 copy-done.2
  426.0 0.7 constant_dynamic-slice_fusion
  426.7 482.5 %all-reduce.7.cloned.1.call-done = f32[6,8,512]{2,1,0:T(8,128)} async-done(((f32[6,8,512]{2,1,0:T(8,128)}), f32[6,8,512]{2,1,0:T(8,128)}) %all-reduce.7.cloned.1.call-update) | async-done | bytes 98320
  909.3 1.4 dynamic-slice_multiply_fusion
  (93 shorter events, 4.8 us)
Async XLA Ops:
  7.2 404.7 %all-reduce.5.cloned.1.call-start = ((), (), s32[]{:S(2)}) async-start(), calls=%async_computation | async-start | bytes 393216 | tf_op jit(solution)/shard_map/psum | solution.py:102
  12.4 0.8 copy-start.8
  114.9 3.6 copy-start.4
  115.0 5.3 copy-start.3
  120.6 3.7 copy-start.5
  120.6 3.7 copy-start.6
  120.6 7.7 copy-start
  120.7 7.7 copy-start.1
  128.4 5.8 copy-start.9
  130.3 778.9 %all-reduce.7.cloned.1.call-start = ((), (), s32[]{:S(2)}) async-start(), calls=%async_computation.1 | async-start | bytes 196608
  135.3 276.6 %copy-start.7 = (bf16[2,12,8,256]{3,2,1,0:T(8,128)(2,1)S(1)}, bf16[2,12,8,256]{3,2,1,0:T(8,128)(2,1)}, u32[]{:S(2)}) copy-start(bf16[2,12,8,256]{3,2,1,0:T(8,128)(2,1)} %param.6) | copy-start | bytes 294916
  425.3 0.7 copy-start.2
Sparse Core Ops, SparseCore 0:
  130.4 72.1 all-reduce.4
  426.1 483.1 all-reduce.6
where the time goes:
time: 918 us
  waiting for transfers between devices  483 us (53%)
  blocking collectives  366 us (40%)
  other arithmetic  24.3 us (3%)
  local copies, waits for them, and re-layouts  23.8 us (3%)
  between operations  20.4 us (2%)
    unnamed x3, waiting for transfers between devices  483 us
    unnamed x1, blocking collectives  269 us
    all_gather x1, blocking collectives, body(): jones_all = lax.all_gather(jones, 'tile', axis=2, tiled=True)  97.3 us
  transfers between devices with their start and end apart: 2, of which 1 were waited for; matrix products, arithmetic and copies ran while one was open for 1% of the time, Pallas kernels for 0%

commit v1 on v0

v1 whole, which is shorter than its diff:
```python
import functools

import jax
import jax.numpy as jnp
from jax import lax
from jax.experimental import pallas as pl
from jax.experimental.pallas import tpu as pltpu
from jax.sharding import PartitionSpec as P

MESH = pl.DeviceIdType.MESH
YH, Z, CORES, DIRS = 4, 8, 2, 8
TILES = YH * Z * CORES
SB = 16
F32 = jnp.float32
BF16 = jnp.bfloat16


def hops(offset):
    y, z, c = offset
    return 2 * min(y, YH - y) + min(z, Z - z) + 0.5 * c


FAR_FIRST = sorted(
    (
        (y, z, c)
        for y in range(YH)
        for z in range(Z)
        for c in range(CORES)
        if (y, z, c) != (0, 0, 0)
    ),
    key=lambda o: -hops(o),
)
Z_NEAR_FIRST = (1, 7, 2, 6, 3, 5, 4)
Z_FAR_FIRST = (4, 3, 5, 2, 6, 1, 7)
YC_FAR_FIRST = ((2, 1), (2, 0), (1, 1), (3, 1), (1, 0), (3, 0), (0, 1))


def times_adjoint(a, b):
    re, im = [], []
    for r in range(2):
        for c in range(2):
            x, y = None, None
            for m in range(2):
                ar, ai, br, bi = a[r * 2 + m], a[4 + r * 2 + m], b[c * 2 + m], b[4 + c * 2 + m]
                xr, xi = ar * br + ai * bi, ai * br - ar * bi
                x, y = (xr, xi) if x is None else (x + xr, y + xi)
            re.append(x)
            im.append(y)
    return re + im


def times(a, b):
    re, im = [], []
    for r in range(2):
        for c in range(2):
            x, y = None, None
            for m in range(2):
                ar, ai, br, bi = a[r * 2 + m], a[4 + r * 2 + m], b[m * 2 + c], b[4 + m * 2 + c]
                xr, xi = ar * br - ai * bi, ar * bi + ai * br
                x, y = (xr, xi) if x is None else (x + xr, y + xi)
            re.append(x)
            im.append(y)
    return re + im


def adjoint_times(a, b):
    re, im = [], []
    for r in range(2):
        for c in range(2):
            x, y = None, None
            for m in range(2):
                ar, ai, br, bi = a[m * 2 + r], a[4 + m * 2 + r], b[m * 2 + c], b[4 + m * 2 + c]
                xr, xi = ar * br + ai * bi, ar * bi - ai * br
                x, y = (xr, xi) if x is None else (x + xr, y + xi)
            re.append(x)
            im.append(y)
    return re + im


def fold(values):
    row = lax.broadcasted_iota(jnp.int32, (8, 128), 0)
    low = row < 4
    first = row % 4 < 2
    a, b, c, d = values
    e = jnp.where(low, a, c) + pltpu.roll(jnp.where(low, c, a), 4, 0)
    f = jnp.where(low, b, d) + pltpu.roll(jnp.where(low, d, b), 4, 0)
    return jnp.where(first, e, pltpu.roll(f, 2, 0)) + jnp.where(first, pltpu.roll(e, 6, 0), f)


def split(x):
    high = x.astype(BF16)
    return high, (x - high.astype(F32)).astype(BF16)


def kernel(
    coherency,
    observed,
    flags,
    tile_map,
    jones,
    res_out,
    grad_out,
    curv_out,
    coh_raw,
    obs_raw,
    rows,
    obs_rows,
    coh,
    gains,
    m_all,
    n_all,
    partial,
    taken,
    residual,
    weight,
    val_p,
    val_q,
    pay,
    paid,
    jones_all,
    stage,
    local_sem,
    send_sem,
    recv_sem,
    near_sem,
):
    tile, me = lax.axis_index("tile"), lax.axis_index("dir")
    y, z, core = tile // (Z * CORES), tile // CORES % Z, tile % CORES

    def at(dy, dz, dc):
        return (
            lax.rem(y + dy, YH) * (Z * CORES)
            + lax.rem(z + dz, Z) * CORES
            + lax.rem(core + dc, CORES)
        )

    def remote(src, dst, send, recv, device):
        return pltpu.make_async_remote_copy(
            src_ref=src,
            dst_ref=dst,
            send_sem=send,
            recv_sem=recv,
            device_id=device,
            device_id_type=MESH,
        )

    get_coh = pltpu.make_async_copy(coherency, coh_raw, local_sem.at[0])
    get_obs = pltpu.make_async_copy(observed, obs_raw, local_sem.at[1])
    get_coh.start()
    get_obs.start()

    barrier = pltpu.get_barrier_semaphore()
    greeted = (
        [(at(0, dz, 0), me) for dz in Z_FAR_FIRST]
        + [(at(dy, 0, dc), me) for dy, dc in YC_FAR_FIRST]
        + [(tile, lax.rem(me + r, DIRS)) for r in range(1, DIRS)]
    )
    for device in greeted:
        pl.semaphore_signal(barrier, inc=1, device_id=device, device_id_type=MESH)

    packed = jnp.zeros((8, 128), F32)
    for k in range(6):
        wide = jnp.concatenate([jones[k], jnp.zeros((8, 120), F32)], axis=1)
        packed = packed + (pltpu.roll(wide, 8 * k, 1) if k else wide)
    packed = packed[0:4] + pltpu.roll(packed, 64, 1)[4:8]
    jones_all[tile] = packed

    get_coh.wait()
    get_obs.wait()

    def to_rows(k, carry):
        for t in range(2):
            for s in range(12):
                block = coh_raw[t, k, s].astype(F32)
                for h in range(2):
                    rows[h, k, pl.ds((s * 2 + t) * 8, 8), :] = block[:, h * 128 : h * 128 + 128]
        for h in range(2):
            for c in range(8):
                coh[k, h, c] = rows[h, k, pl.ds(c, 24, stride=8), :].reshape(3, 8, 128)
        return carry

    lax.fori_loop(0, 6, to_rows, 0)
    for t in range(2):
        for s in range(12):
            block = obs_raw[t, s].astype(F32)
            for h in range(2):
                obs_rows[h, pl.ds((s * 2 + t) * 8, 8), :] = block[:, h * 128 : h * 128 + 128]

    odd_row = lax.broadcasted_iota(jnp.int32, (8, 128), 0) % 2 == 1
    for h in range(2):
        baseline = lax.broadcasted_iota(jnp.int32, (8, 128), 1) + 128 * h
        upper = jnp.where(baseline // SB < baseline % SB, 1, 0)
        for g in range(3):
            both = []
            for t in range(2):
                ahead = jnp.where(tile_map[t, 0] < tile_map[t, 1], 1, 0)
                kept = 1 - flags[t, g]
                both.append((jnp.maximum(upper, ahead) * kept).astype(F32))
            weight[h, g] = jnp.where(odd_row, both[1], both[0])

    pl.semaphore_wait(barrier, len(greeted))

    mine = jones_all.at[tile]
    for dz in Z_FAR_FIRST:
        remote(mine, mine, send_sem.at[0], near_sem.at[dz], (at(0, dz, 0), me)).start()
    for dy, dc in YC_FAR_FIRST:
        remote(mine, mine, send_sem.at[0], recv_sem.at[0], (at(dy, 0, dc), me)).start()
    for dz in Z_NEAR_FIRST:
        piece = jones_all.at[at(0, Z - dz, 0)]
        remote(piece, piece, send_sem.at[0], near_sem.at[dz], (at(0, dz, 0), me)).wait_recv()
        for dy, dc in YC_FAR_FIRST:
            remote(piece, piece, send_sem.at[0], recv_sem.at[0], (at(dy, 0, dc), me)).start()
    count = 7 * Z
    far = jones_all.at[pl.ds(0, count)]
    remote(far, far, send_sem.at[0], recv_sem.at[0], (at(1, 0, 0), me)).wait_recv()

    row = lax.broadcasted_iota(jnp.int32, (6, 8, 256), 1)
    direction = lax.broadcasted_iota(jnp.int32, (6, 8, 256), 0)
    lane = lax.broadcasted_iota(jnp.int32, (6, 8, 256), 2)
    own = lane % 128 // 8 == row // 4 * 8 + direction
    station = lax.broadcasted_iota(jnp.int32, (256, 256), 0)
    station = station // 128 * 8 + station % 8
    baseline = lax.broadcasted_iota(jnp.int32, (256, 256), 1)
    for side in range(2):
        spread = jnp.where(station == (baseline % SB if side else baseline // SB), 1.0, 0.0)
        spread = spread.astype(BF16)
        for t in range(2):
            block = tile_map[t, side]
            both = jnp.concatenate([jones_all[2 * block], jones_all[2 * block + 1]], axis=1)
            both = jnp.concatenate([both, both], axis=0)
            chosen = jnp.where(own, both[None], 0.0).reshape(48, 256)
            high, low = split(chosen)
            full = jnp.dot(high, spread, preferred_element_type=F32)
            full = full + jnp.dot(low, spread, preferred_element_type=F32)
            for h in range(2):
                gains[side, t, h] = full[:, h * 128 : h * 128 + 128].reshape(6, 8, 128)

    def gain(side, k, h):
        return [
            jnp.where(
                odd_row,
                jnp.broadcast_to(gains[side, 1, h, k, pl.ds(c, 1), :], (8, 128)),
                jnp.broadcast_to(gains[side, 0, h, k, pl.ds(c, 1), :], (8, 128)),
            )
            for c in range(8)
        ]

    for h in range(2):

        def add_direction(k, total, h=h):
            p, q = gain(0, k, h), gain(1, k, h)
            out = []
            for g in range(3):
                m = times_adjoint([coh[k, h, c, g] for c in range(8)], q)
                for c in range(8):
                    m_all[k, h, c, g] = m[c]
                v = times(p, m)
                out += [total[g * 8 + c] + v[c] for c in range(8)]
            return tuple(out)

        total = lax.fori_loop(0, 6, add_direction, (jnp.zeros((8, 128), F32),) * 24)
        for g in range(3):
            for c in range(8):
                partial[c, h, g] = total[g * 8 + c]

    for r in range(1, DIRS):
        other = lax.rem(me + r, DIRS)
        remote(
            partial.at[other], taken.at[r - 1], send_sem.at[1], recv_sem.at[1], (tile, other)
        ).start()

    val_p[...] = jnp.zeros_like(val_p)
    val_q[...] = jnp.zeros_like(val_q)
    for h in range(2):

        def two_directions(pair, carry, h=h):
            rows_p, rows_q = [], []
            for j in range(2):
                k = pair * 2 + j
                p = gain(0, k, h)
                cp, cq = [0.0, 0.0], [0.0, 0.0]
                for g in range(3):
                    n = times(p, [coh[k, h, c, g] for c in range(8)])
                    for c in range(8):
                        n_all[k, h, c, g] = n[c]
                    m = [m_all[k, h, c, g] for c in range(8)]
                    w = weight[h, g]
                    for c in range(2):
                        cp[c] = cp[c] + w * sum(m[e] * m[e] for e in (2 * c, 2 * c + 1, 4 + 2 * c, 5 + 2 * c))
                        cq[c] = cq[c] + w * sum(n[e] * n[e] for e in (c, c + 2, c + 4, c + 6))
                rows_p += cp
                rows_q += cq
            val_p[12 + pair, :, h * 128 : h * 128 + 128] = fold(rows_p)
            val_q[12 + pair, :, h * 128 : h * 128 + 128] = fold(rows_q)
            return carry

        lax.fori_loop(0, 3, two_directions, 0)

    remote(taken, taken, send_sem.at[1], recv_sem.at[1], (tile, me)).wait_recv()
    for h in range(2):
        model = partial[me, h]
        for r in range(DIRS - 1):
            model = model + taken[r, h]
        seen = obs_rows[h, pl.ds(me, 24, stride=8), :].reshape(3, 8, 128)
        residual[me, h] = weight[h] * (seen - model)

    for r in range(1, DIRS):
        other = lax.rem(me + r, DIRS)
        remote(
            residual.at[me], residual.at[me], send_sem.at[2], recv_sem.at[2], (tile, other)
        ).start()
    seven = residual.at[pl.ds(0, DIRS - 1)]
    remote(seven, seven, send_sem.at[2], recv_sem.at[2], (tile, me)).wait_recv()

    for h in range(2):

        def one_direction(k, carry, h=h):
            a, b = None, None
            for g in range(3):
                res = [residual[c, h, g] for c in range(8)]
                u = times_adjoint(res, [m_all[k, h, c, g] for c in range(8)])
                v = adjoint_times(res, [n_all[k, h, c, g] for c in range(8)])
                a = u if a is None else [i + j for i, j in zip(a, u)]
                b = v if b is None else [i + j for i, j in zip(b, v)]
            for j in range(2):
                val_p[2 * k + j, :, h * 128 : h * 128 + 128] = fold(a[4 * j : 4 * j + 4])
                val_q[2 * k + j, :, h * 128 : h * 128 + 128] = fold(b[4 * j : 4 * j + 4])
            return carry

        lax.fori_loop(0, 6, one_direction, 0)

    place = lax.broadcasted_iota(jnp.int32, (16, 256), 0)
    place = place // 8 * 4 + place // 4 % 2 * 8 + place % 4
    baseline = lax.broadcasted_iota(jnp.int32, (16, 256), 1)
    even = lax.broadcasted_iota(jnp.int32, (8, 128), 1) % 2 == 0
    parts = []
    for side, val in ((0, val_p), (1, val_q)):
        gather = jnp.where(place == (baseline % SB if side else baseline // SB), 1.0, 0.0)
        gather = gather.astype(BF16)
        high, low = split(val[...].reshape(128, 256))
        dims = (((1,), (1,)), ((), ()))
        sums = lax.dot_general(gather, high, dims, preferred_element_type=F32)
        sums = sums + lax.dot_general(gather, low, dims, preferred_element_type=F32)
        top, bottom = sums[0:8], sums[8:16]
        parts.append(
            (
                side,
                0,
                jnp.where(even, top, 0.0) + pltpu.roll(jnp.where(even, bottom, 0.0), 1, 1),
            )
        )
        parts.append(
            (
                side,
                1,
                pltpu.roll(jnp.where(even, 0.0, top), 127, 1) + jnp.where(even, 0.0, bottom),
            )
        )

    for b in range(TILES // 2):
        block = jnp.zeros((8, 128), F32)
        for side, t, part in parts:
            block = block + jnp.where(tile_map[t, side] == b, part, 0.0)
        pay[2 * b] = block[0:4]
        pay[2 * b + 1] = block[4:8]

    for number, (dy, dz, dc) in enumerate(FAR_FIRST):
        owner = at(dy, dz, dc)
        remote(
            pay.at[owner], paid.at[number], send_sem.at[3], recv_sem.at[3], (owner, me)
        ).start()

    half, part = me // 4, me % 4
    for c in range(8):
        wide = residual[c, half].reshape(24, 128)
        wide = pltpu.roll(wide, lax.rem(128 - 32 * part, 128), 1)
        stage[pl.ds(c, 24, stride=8), :] = wide
    for t in range(2):
        for s in range(12):
            res_out[t, s] = stage[pl.ds((s * 2 + t) * 8, 8), 0:32]

    remote(paid, paid, send_sem.at[3], recv_sem.at[3], (tile, me)).wait_recv()
    total = pay[tile] + jnp.sum(paid[...], axis=0)
    wide = jnp.concatenate([total, pltpu.roll(total, 127, 1)], axis=0) * (1.0 / (12 * SB))
    pick = jnp.where(
        lax.broadcasted_iota(jnp.int32, (64, 128), 1)
        == 2 * lax.broadcasted_iota(jnp.int32, (64, 128), 0),
        1.0,
        0.0,
    ).astype(BF16)
    high, low = split(wide)
    rest = (wide - high.astype(F32) - low.astype(F32)).astype(BF16)
    dims = (((1,), (1,)), ((), ()))
    owned = sum(
        lax.dot_general(pick, x, dims, preferred_element_type=F32) for x in (high, low, rest)
    )
    grad_out[...] = owned[0:48].reshape(6, 8, 8)
    for k in range(6):
        curv_out[k] = owned[48 + 2 * k : 50 + 2 * k]

    sent = jones_all.at[pl.ds(0, TILES - 1)]
    remote(sent, sent, send_sem.at[0], recv_sem.at[0], (tile, me)).wait_send()
    remote(taken, taken, send_sem.at[1], recv_sem.at[1], (tile, me)).wait_send()
    remote(seven, seven, send_sem.at[2], recv_sem.at[2], (tile, me)).wait_send()
    remote(paid, paid, send_sem.at[3], recv_sem.at[3], (tile, me)).wait_send()


def body(coherency, observed, flags, tile_map, jones):
    vmem, smem, anywhere = (
        pl.BlockSpec(memory_space=m) for m in (pltpu.VMEM, pltpu.SMEM, pl.ANY)
    )
    scratch = [
        pltpu.VMEM((2, 6, 12, 8, 256), BF16),
        pltpu.VMEM((2, 12, 8, 256), BF16),
        pltpu.VMEM((2, 6, 192, 128), F32),
        pltpu.VMEM((2, 192, 128), F32),
        pltpu.VMEM((6, 2, 8, 3, 8, 128), F32),
        pltpu.VMEM((2, 2, 2, 6, 8, 128), F32),
        pltpu.VMEM((6, 2, 8, 3, 8, 128), F32),
        pltpu.VMEM((6, 2, 8, 3, 8, 128), F32),
        pltpu.VMEM((8, 2, 3, 8, 128), F32),
        pltpu.VMEM((7, 2, 3, 8, 128), F32),
        pltpu.VMEM((8, 2, 3, 8, 128), F32),
        pltpu.VMEM((2, 3, 8, 128), F32),
        pltpu.VMEM((16, 8, 256), F32),
        pltpu.VMEM((16, 8, 256), F32),
        pltpu.VMEM((TILES, 4, 128), F32),
        pltpu.VMEM((TILES - 1, 4, 128), F32),
        pltpu.VMEM((TILES, 4, 128), F32),
        pltpu.VMEM((192, 128), F32),
        pltpu.SemaphoreType.DMA((2,)),
        pltpu.SemaphoreType.DMA((4,)),
        pltpu.SemaphoreType.DMA((4,)),
        pltpu.SemaphoreType.DMA((Z,)),
    ]
    return pl.pallas_call(
        kernel,
        out_shape=(
            jax.ShapeDtypeStruct((2, 12, 8, 32), F32),
            jax.ShapeDtypeStruct((6, 8, 8), F32),
            jax.ShapeDtypeStruct((6, 2, 8), F32),
        ),
        in_specs=[anywhere, anywhere, smem, smem, vmem],
        out_specs=(vmem, vmem, vmem),
        scratch_shapes=scratch,
        compiler_params=pltpu.CompilerParams(
            collective_id=0, has_side_effects=True, vmem_limit_bytes=40 * 1024 * 1024
        ),
    )(coherency, observed, flags, tile_map, jones)


def solution(mesh):
    return jax.shard_map(
        body,
        mesh=mesh,
        in_specs=(
            P("tile", "dir", None, None, None),
            P("tile", None, None, None),
            P("tile", None),
            P("tile", None),
            P("dir", None, "tile"),
        ),
        out_specs=(P("tile", None, None, "dir"), P("dir", None, "tile"), P("dir", None, "tile")),
        check_vma=False,
    )
```

time: 918 us -> 50.8 us (0.06)
  waiting for transfers between devices: 483 us -> 0 us
  blocking collectives: 366 us -> 0 us
  Pallas kernels: 0 us -> 43.9 us
  other arithmetic: 24.3 us -> 0 us
  between operations: 20.4 us -> 0.65 us
  local copies, waits for them, and re-layouts: 23.8 us -> 5.89 us
    unnamed x3 -> x0, waiting for transfers between devices: 483 us -> none
    unnamed x1 -> x0, blocking collectives: 269 us -> none
    all_gather x1 -> x0, blocking collectives: 97.3 us -> none  [body(): jones_all = lax.all_gather(jones, 'tile', axis=2, tiled=True)]
    pallas_call x0 -> x1, Pallas kernels: none -> 43.9 us  [body(): pl.pallas_call(kernel, out_shape=(jax.ShapeDtypeStruct((2, 12, 8, 32), F3...]
    reduce_sum x28 -> x0, other arithmetic: 18.5 us -> none  [the longest x8 14.1 us: complex_product(): jnp.sum(lre * rre - lim * rim, axis=-3)]
  transfers between devices with their start and end apart: 2 -> 0, of which waited for: 1 -> 0; matrix products, arithmetic and copies ran while one was open for 1% -> 0% of each run, Pallas kernels for 0% -> 0%
where the time goes in v1:
time: 50.8 us; the launch traced here: 50.5 us
  Pallas kernels  43.9 us (86%)
  local copies, waits for them, and re-layouts  5.89 us (12%)
  between operations  0.65 us (1%)
    pallas_call x1, Pallas kernels, body(): pl.pallas_call(kernel, out_shape=(jax.ShapeDtypeStruct((2, 12, 8, 32), F3...  43.9 us
    unnamed x13, local copies, waits for them, and re-layouts  5.89 us

profile of v1, /device:TPU:1, one launch (start us, length us, event | category | flops | bytes accessed | tf_op | source)
XLA Modules:
  0.0 50.5 jit_solution(15142784245545138620)
XLA Ops:
  0.6 0.0 copy-start
  0.6 1.1 %copy-done = bf16[2,6,12,8,256]{4,3,2,1,0:T(8,128)(2,1)S(1)} copy-done((bf16[2,6,12,8,256]{4,3,2,1,0:T(8,128)(2,1)S(1)}, bf16[2,6,12,8,256]{4,3,2,1,0:T(8,128)(2,1)}, u32[]{:S(2)}) %copy-start) | copy-done | bytes 589848
  1.7 0.0 copy-start.1
  1.7 0.9 %copy-done.1 = bf16[2,12,8,256]{3,2,1,0:T(8,128)(2,1)S(1)} copy-done((bf16[2,12,8,256]{3,2,1,0:T(8,128)(2,1)S(1)}, bf16[2,12,8,256]{3,2,1,0:T(8,128)(2,1)}, u32[]{:S(2)}) %copy-start.1) | copy-done | bytes 98328
  2.6 0.0 copy-start.2
  2.6 0.7 %copy-done.2 = f32[6,8,8]{2,1,0:T(8,128)S(1)} copy-done((f32[6,8,8]{2,1,0:T(8,128)S(1)}, f32[6,8,8]{2,1,0:T(8,128)}, u32[]{:S(2)}) %copy-start.2) | copy-done | bytes 1560
  3.3 0.0 copy-start.3
  3.3 0.7 %copy-done.3 = s32[2,3]{1,0:T(2,128)S(1)} copy-done((s32[2,3]{1,0:T(2,128)S(1)}, s32[2,3]{1,0:T(2,128)}, u32[]{:S(2)}) %copy-start.3) | copy-done | bytes 48
  4.0 0.0 copy-start.4
  4.0 0.7 %copy-done.4 = s32[2,2]{1,0:T(2,128)S(1)} copy-done((s32[2,2]{1,0:T(2,128)S(1)}, s32[2,2]{1,0:T(2,128)}, u32[]{:S(2)}) %copy-start.4) | copy-done | bytes 40
  4.7 43.9 %shard_map.76 = (f32[2,12,8,32]{3,2,1,0:T(8,128)S(1)}, f32[6,8,8]{2,1,0:T(8,128)S(1)}, f32[6,2,8]{2,1,0:T(2,128)S(1)}) custom-call(bf16[2,6,12,8,256]{4,3,2,1,0:T(8,128)(2,1)S(1)} %copy-done, bf16[2,12,8,256]{3,2,1,0:T(8,128)(2,1)S(1)} %copy-done.1, s32[2,3]{1,0:T(2,128)S(1)} %copy-done.3, s32[2,2]{1,0:T(2,128)S(1)} %copy-done.4, f32[6,8,8]{2,1,0:T(8,128)S(1)} %copy-done.2), custom_call_target="tpu_custom_call" | custom-call | tf_op jit(solution)/shard_map/pallas_call | solution.py:436
  48.6 0.6 %copy.11 = f32[2,12,8,32]{3,2,1,0:T(8,128)} copy(f32[2,12,8,32]{3,2,1,0:T(8,128)S(1)} %get-tuple-element.6) | data formatting | bytes 49152
  49.3 0.6 %copy.12 = f32[6,8,8]{2,1,0:T(8,128)} copy(f32[6,8,8]{2,1,0:T(8,128)S(1)} %get-tuple-element.7) | data formatting | bytes 3072
  49.9 0.6 %copy.13 = f32[6,2,8]{2,1,0:T(2,128)} copy(f32[6,2,8]{2,1,0:T(2,128)S(1)} %get-tuple-element.8) | data formatting | bytes 768
Async XLA Ops:
  0.6 1.1 %copy-start = (bf16[2,6,12,8,256]{4,3,2,1,0:T(8,128)(2,1)S(1)}, bf16[2,6,12,8,256]{4,3,2,1,0:T(8,128)(2,1)}, u32[]{:S(2)}) copy-start(bf16[2,6,12,8,256]{4,3,2,1,0:T(8,128)(2,1)} %coherency.1) | copy-start | bytes 1769476
  1.7 0.9 %copy-start.1 = (bf16[2,12,8,256]{3,2,1,0:T(8,128)(2,1)S(1)}, bf16[2,12,8,256]{3,2,1,0:T(8,128)(2,1)}, u32[]{:S(2)}) copy-start(bf16[2,12,8,256]{3,2,1,0:T(8,128)(2,1)} %observed.1) | copy-start | bytes 294916
  2.6 0.7 %copy-start.2 = (f32[6,8,8]{2,1,0:T(8,128)S(1)}, f32[6,8,8]{2,1,0:T(8,128)}, u32[]{:S(2)}) copy-start(f32[6,8,8]{2,1,0:T(8,128)} %jones.1) | copy-start | bytes 4612
  3.3 0.7 %copy-start.3 = (s32[2,3]{1,0:T(2,128)S(1)}, s32[2,3]{1,0:T(2,128)}, u32[]{:S(2)}) copy-start(s32[2,3]{1,0:T(2,128)} %flags.1) | copy-start | bytes 76
  4.0 0.7 %copy-start.4 = (s32[2,2]{1,0:T(2,128)S(1)}, s32[2,2]{1,0:T(2,128)}, u32[]{:S(2)}) copy-start(s32[2,2]{1,0:T(2,128)} %tile_map.1) | copy-start | bytes 52

commit v2 on v1

--- a/solution.py
+++ b/solution.py
@@ -79,12 +79,15 @@
 
 def fold(values):
     row = lax.broadcasted_iota(jnp.int32, (8, 128), 0)
-    low = row < 4
-    first = row % 4 < 2
+    first, even = row % 4 < 2, row % 2 == 0
     a, b, c, d = values
-    e = jnp.where(low, a, c) + pltpu.roll(jnp.where(low, c, a), 4, 0)
-    f = jnp.where(low, b, d) + pltpu.roll(jnp.where(low, d, b), 4, 0)
-    return jnp.where(first, e, pltpu.roll(f, 2, 0)) + jnp.where(first, pltpu.roll(e, 6, 0), f)
+    e = jnp.where(first, a, pltpu.roll(c, 2, 0)) + jnp.where(first, pltpu.roll(a, 6, 0), c)
+    f = jnp.where(first, b, pltpu.roll(d, 2, 0)) + jnp.where(first, pltpu.roll(b, 6, 0), d)
+    return jnp.where(even, e, pltpu.roll(f, 1, 0)) + jnp.where(even, pltpu.roll(e, 7, 0), f)
+
+
+def row_of(t, s):
+    return s // 4 * 8 + t * 4 + s % 4
 
 
 def split(x):
@@ -95,9 +98,9 @@
 def kernel(
     coherency,
     observed,
-    flags,
-    tile_map,
-    jones,
+    flags_in,
+    tile_map_in,
+    jones_in,
     res_out,
     grad_out,
     curv_out,
@@ -119,6 +122,10 @@
     paid,
     jones_all,
     stage,
+    collect,
+    flags,
+    tile_map,
+    jones,
     local_sem,
     send_sem,
     recv_sem,
@@ -144,11 +151,6 @@
             device_id_type=MESH,
         )
 
-    get_coh = pltpu.make_async_copy(coherency, coh_raw, local_sem.at[0])
-    get_obs = pltpu.make_async_copy(observed, obs_raw, local_sem.at[1])
-    get_coh.start()
-    get_obs.start()
-
     barrier = pltpu.get_barrier_semaphore()
     greeted = (
         [(at(0, dz, 0), me) for dz in Z_FAR_FIRST]
@@ -158,6 +160,22 @@
     for device in greeted:
         pl.semaphore_signal(barrier, inc=1, device_id=device, device_id_type=MESH)
 
+    here = [
+        pltpu.make_async_copy(src, dst, local_sem.at[number])
+        for number, (src, dst) in enumerate(
+            (
+                (jones_in, jones),
+                (flags_in, flags),
+                (tile_map_in, tile_map),
+                (coherency, coh_raw),
+                (observed, obs_raw),
+            )
+        )
+    ]
+    for copy in here:
+        copy.start()
+
+    here[0].wait()
     packed = jnp.zeros((8, 128), F32)
     for k in range(6):
         wide = jnp.concatenate([jones[k], jnp.zeros((8, 120), F32)], axis=1)
@@ -165,15 +183,22 @@
     packed = packed[0:4] + pltpu.roll(packed, 64, 1)[4:8]
     jones_all[tile] = packed
 
-    get_coh.wait()
-    get_obs.wait()
+    pl.semaphore_wait(barrier, len(greeted))
+
+    mine = jones_all.at[tile]
+    for dz in Z_FAR_FIRST:
+        remote(mine, mine, send_sem.at[0], near_sem.at[dz], (at(0, dz, 0), me)).start()
+    for dy, dc in YC_FAR_FIRST:
+        remote(mine, mine, send_sem.at[0], recv_sem.at[0], (at(dy, 0, dc), me)).start()
+    for copy in here[1:]:
+        copy.wait()
 
     def to_rows(k, carry):
         for t in range(2):
             for s in range(12):
                 block = coh_raw[t, k, s].astype(F32)
                 for h in range(2):
-                    rows[h, k, pl.ds((s * 2 + t) * 8, 8), :] = block[:, h * 128 : h * 128 + 128]
+                    rows[h, k, pl.ds(row_of(t, s) * 8, 8), :] = block[:, h * 128 : h * 128 + 128]
         for h in range(2):
             for c in range(8):
                 coh[k, h, c] = rows[h, k, pl.ds(c, 24, stride=8), :].reshape(3, 8, 128)
@@ -184,9 +209,9 @@
         for s in range(12):
             block = obs_raw[t, s].astype(F32)
             for h in range(2):
-                obs_rows[h, pl.ds((s * 2 + t) * 8, 8), :] = block[:, h * 128 : h * 128 + 128]
-
-    odd_row = lax.broadcasted_iota(jnp.int32, (8, 128), 0) % 2 == 1
+                obs_rows[h, pl.ds(row_of(t, s) * 8, 8), :] = block[:, h * 128 : h * 128 + 128]
+
+    second = lax.broadcasted_iota(jnp.int32, (8, 128), 0) >= 4
     for h in range(2):
         baseline = lax.broadcasted_iota(jnp.int32, (8, 128), 1) + 128 * h
         upper = jnp.where(baseline // SB < baseline % SB, 1, 0)
@@ -196,15 +221,17 @@
                 ahead = jnp.where(tile_map[t, 0] < tile_map[t, 1], 1, 0)
                 kept = 1 - flags[t, g]
                 both.append((jnp.maximum(upper, ahead) * kept).astype(F32))
-            weight[h, g] = jnp.where(odd_row, both[1], both[0])
-
-    pl.semaphore_wait(barrier, len(greeted))
-
-    mine = jones_all.at[tile]
-    for dz in Z_FAR_FIRST:
-        remote(mine, mine, send_sem.at[0], near_sem.at[dz], (at(0, dz, 0), me)).start()
-    for dy, dc in YC_FAR_FIRST:
-        remote(mine, mine, send_sem.at[0], recv_sem.at[0], (at(dy, 0, dc), me)).start()
+            weight[h, g] = jnp.where(second, both[1], both[0])
+
+    baseline = lax.broadcasted_iota(jnp.int32, (256, 256), 0)
+    station = lax.broadcasted_iota(jnp.int32, (256, 256), 1)
+    station = station // 128 * 8 + station % 8
+    for side in range(2):
+        own = station == (baseline % SB if side else baseline // SB)
+        collect[side] = jnp.where(own, 1.0, 0.0).astype(BF16)
+    val_p[15] = jnp.zeros((8, 256), F32)
+    val_q[15] = jnp.zeros((8, 256), F32)
+
     for dz in Z_NEAR_FIRST:
         piece = jones_all.at[at(0, Z - dz, 0)]
         remote(piece, piece, send_sem.at[0], near_sem.at[dz], (at(0, dz, 0), me)).wait_recv()
@@ -238,7 +265,7 @@
     def gain(side, k, h):
         return [
             jnp.where(
-                odd_row,
+                second,
                 jnp.broadcast_to(gains[side, 1, h, k, pl.ds(c, 1), :], (8, 128)),
                 jnp.broadcast_to(gains[side, 0, h, k, pl.ds(c, 1), :], (8, 128)),
             )
@@ -263,14 +290,16 @@
             for c in range(8):
                 partial[c, h, g] = total[g * 8 + c]
 
-    for r in range(1, DIRS):
-        other = lax.rem(me + r, DIRS)
-        remote(
-            partial.at[other], taken.at[r - 1], send_sem.at[1], recv_sem.at[1], (tile, other)
-        ).start()
-
-    val_p[...] = jnp.zeros_like(val_p)
-    val_q[...] = jnp.zeros_like(val_q)
+        for r in range(1, DIRS):
+            other = lax.rem(me + r, DIRS)
+            remote(
+                partial.at[other, h],
+                taken.at[h, r - 1],
+                send_sem.at[1],
+                recv_sem.at[1 + h],
+                (tile, other),
+            ).start()
+
     for h in range(2):
 
         def two_directions(pair, carry, h=h):
@@ -296,28 +325,27 @@
 
         lax.fori_loop(0, 3, two_directions, 0)
 
-    remote(taken, taken, send_sem.at[1], recv_sem.at[1], (tile, me)).wait_recv()
     for h in range(2):
+        got = taken.at[h]
+        remote(got, got, send_sem.at[1], recv_sem.at[1 + h], (tile, me)).wait_recv()
         model = partial[me, h]
         for r in range(DIRS - 1):
-            model = model + taken[r, h]
+            model = model + taken[h, r]
         seen = obs_rows[h, pl.ds(me, 24, stride=8), :].reshape(3, 8, 128)
-        residual[me, h] = weight[h] * (seen - model)
-
-    for r in range(1, DIRS):
-        other = lax.rem(me + r, DIRS)
-        remote(
-            residual.at[me], residual.at[me], send_sem.at[2], recv_sem.at[2], (tile, other)
-        ).start()
-    seven = residual.at[pl.ds(0, DIRS - 1)]
-    remote(seven, seven, send_sem.at[2], recv_sem.at[2], (tile, me)).wait_recv()
+        residual[h, me] = weight[h] * (seen - model)
+        done = residual.at[h, me]
+        for r in range(1, DIRS):
+            other = lax.rem(me + r, DIRS)
+            remote(done, done, send_sem.at[2], recv_sem.at[3 + h], (tile, other)).start()
 
     for h in range(2):
+        got = residual.at[h, pl.ds(0, DIRS - 1)]
+        remote(got, got, send_sem.at[2], recv_sem.at[3 + h], (tile, me)).wait_recv()
 
         def one_direction(k, carry, h=h):
             a, b = None, None
             for g in range(3):
-                res = [residual[c, h, g] for c in range(8)]
+                res = [residual[h, c, g] for c in range(8)]
                 u = times_adjoint(res, [m_all[k, h, c, g] for c in range(8)])
                 v = adjoint_times(res, [n_all[k, h, c, g] for c in range(8)])
                 a = u if a is None else [i + j for i, j in zip(a, u)]
@@ -329,33 +357,21 @@
 
         lax.fori_loop(0, 6, one_direction, 0)
 
-    place = lax.broadcasted_iota(jnp.int32, (16, 256), 0)
-    place = place // 8 * 4 + place // 4 % 2 * 8 + place % 4
-    baseline = lax.broadcasted_iota(jnp.int32, (16, 256), 1)
-    even = lax.broadcasted_iota(jnp.int32, (8, 128), 1) % 2 == 0
+    group = lax.broadcasted_iota(jnp.int32, (8, 128), 1) // 8
     parts = []
     for side, val in ((0, val_p), (1, val_q)):
-        gather = jnp.where(place == (baseline % SB if side else baseline // SB), 1.0, 0.0)
-        gather = gather.astype(BF16)
         high, low = split(val[...].reshape(128, 256))
-        dims = (((1,), (1,)), ((), ()))
-        sums = lax.dot_general(gather, high, dims, preferred_element_type=F32)
-        sums = sums + lax.dot_general(gather, low, dims, preferred_element_type=F32)
-        top, bottom = sums[0:8], sums[8:16]
-        parts.append(
-            (
-                side,
-                0,
-                jnp.where(even, top, 0.0) + pltpu.roll(jnp.where(even, bottom, 0.0), 1, 1),
-            )
-        )
-        parts.append(
-            (
-                side,
-                1,
-                pltpu.roll(jnp.where(even, 0.0, top), 127, 1) + jnp.where(even, 0.0, bottom),
-            )
-        )
+        sums = jnp.dot(high, collect[side], preferred_element_type=F32)
+        sums = sums + jnp.dot(low, collect[side], preferred_element_type=F32)
+        sums = sums.reshape(16, 8, 256)
+        halves = []
+        for h in range(2):
+            piece = jnp.zeros((8, 128), F32)
+            for g in range(15):
+                piece = jnp.where(group == g, sums[g, :, h * 128 : h * 128 + 128], piece)
+            halves.append(piece)
+        parts.append((side, 0, jnp.where(second, pltpu.roll(halves[1], 4, 0), halves[0])))
+        parts.append((side, 1, jnp.where(second, halves[1], pltpu.roll(halves[0], 4, 0))))
 
     for b in range(TILES // 2):
         block = jnp.zeros((8, 128), F32)
@@ -367,48 +383,37 @@
     for number, (dy, dz, dc) in enumerate(FAR_FIRST):
         owner = at(dy, dz, dc)
         remote(
-            pay.at[owner], paid.at[number], send_sem.at[3], recv_sem.at[3], (owner, me)
+            pay.at[owner], paid.at[number], send_sem.at[3], recv_sem.at[5], (owner, me)
         ).start()
 
     half, part = me // 4, me % 4
     for c in range(8):
-        wide = residual[c, half].reshape(24, 128)
+        wide = residual[half, c].reshape(24, 128)
         wide = pltpu.roll(wide, lax.rem(128 - 32 * part, 128), 1)
         stage[pl.ds(c, 24, stride=8), :] = wide
     for t in range(2):
         for s in range(12):
-            res_out[t, s] = stage[pl.ds((s * 2 + t) * 8, 8), 0:32]
-
-    remote(paid, paid, send_sem.at[3], recv_sem.at[3], (tile, me)).wait_recv()
-    total = pay[tile] + jnp.sum(paid[...], axis=0)
-    wide = jnp.concatenate([total, pltpu.roll(total, 127, 1)], axis=0) * (1.0 / (12 * SB))
-    pick = jnp.where(
-        lax.broadcasted_iota(jnp.int32, (64, 128), 1)
-        == 2 * lax.broadcasted_iota(jnp.int32, (64, 128), 0),
-        1.0,
-        0.0,
-    ).astype(BF16)
-    high, low = split(wide)
-    rest = (wide - high.astype(F32) - low.astype(F32)).astype(BF16)
-    dims = (((1,), (1,)), ((), ()))
-    owned = sum(
-        lax.dot_general(pick, x, dims, preferred_element_type=F32) for x in (high, low, rest)
-    )
-    grad_out[...] = owned[0:48].reshape(6, 8, 8)
+            res_out[t, s] = stage[pl.ds(row_of(t, s) * 8, 8), 0:32]
+
+    remote(paid, paid, send_sem.at[3], recv_sem.at[5], (tile, me)).wait_recv()
+    terms = [pay[tile]] + [paid[number] for number in range(TILES - 1)]
+    while len(terms) > 1:
+        terms = [a + b for a, b in zip(terms[::2], terms[1::2])]
+    total = terms[0] * (1.0 / (12 * SB))
+    moved = [(pltpu.roll(total, 128 - 8 * g, 1) if g else total)[:, 0:8] for g in range(15)]
     for k in range(6):
-        curv_out[k] = owned[48 + 2 * k : 50 + 2 * k]
+        grad_out[k] = jnp.concatenate(moved[2 * k : 2 * k + 2], axis=0)
+        curv_out[k] = moved[12 + k // 2][k % 2 * 2 : k % 2 * 2 + 2]
 
     sent = jones_all.at[pl.ds(0, TILES - 1)]
     remote(sent, sent, send_sem.at[0], recv_sem.at[0], (tile, me)).wait_send()
     remote(taken, taken, send_sem.at[1], recv_sem.at[1], (tile, me)).wait_send()
-    remote(seven, seven, send_sem.at[2], recv_sem.at[2], (tile, me)).wait_send()
-    remote(paid, paid, send_sem.at[3], recv_sem.at[3], (tile, me)).wait_send()
+    remote(taken, taken, send_sem.at[2], recv_sem.at[1], (tile, me)).wait_send()
+    remote(paid, paid, send_sem.at[3], recv_sem.at[5], (tile, me)).wait_send()
 
 
 def body(coherency, observed, flags, tile_map, jones):
-    vmem, smem, anywhere = (
-        pl.BlockSpec(memory_space=m) for m in (pltpu.VMEM, pltpu.SMEM, pl.ANY)
-    )
+    vmem, hbm = (pl.BlockSpec(memory_space=m) for m in (pltpu.VMEM, pltpu.HBM))
     scratch = [
         pltpu.VMEM((2, 6, 12, 8, 256), BF16),
         pltpu.VMEM((2, 12, 8, 256), BF16),
@@ -419,8 +424,8 @@
         pltpu.VMEM((6, 2, 8, 3, 8, 128), F32),
         pltpu.VMEM((6, 2, 8, 3, 8, 128), F32),
         pltpu.VMEM((8, 2, 3, 8, 128), F32),
-        pltpu.VMEM((7, 2, 3, 8, 128), F32),
-        pltpu.VMEM((8, 2, 3, 8, 128), F32),
+        pltpu.VMEM((2, 7, 3, 8, 128), F32),
+        pltpu.VMEM((2, 8, 3, 8, 128), F32),
         pltpu.VMEM((2, 3, 8, 128), F32),
         pltpu.VMEM((16, 8, 256), F32),
         pltpu.VMEM((16, 8, 256), F32),
@@ -428,9 +433,13 @@
         pltpu.VMEM((TILES - 1, 4, 128), F32),
         pltpu.VMEM((TILES, 4, 128), F32),
         pltpu.VMEM((192, 128), F32),
-        pltpu.SemaphoreType.DMA((2,)),
+        pltpu.VMEM((2, 256, 256), BF16),
+        pltpu.SMEM((2, 3), jnp.int32),
+        pltpu.SMEM((2, 2), jnp.int32),
+        pltpu.VMEM((6, 8, 8), F32),
+        pltpu.SemaphoreType.DMA((5,)),
         pltpu.SemaphoreType.DMA((4,)),
-        pltpu.SemaphoreType.DMA((4,)),
+        pltpu.SemaphoreType.DMA((6,)),
         pltpu.SemaphoreType.DMA((Z,)),
     ]
     return pl.pallas_call(
@@ -440,13 +449,13 @@
             jax.ShapeDtypeStruct((6, 8, 8), F32),
             jax.ShapeDtypeStruct((6, 2, 8), F32),
         ),
-        in_specs=[anywhere, anywhere, smem, smem, vmem],
+        in_specs=[hbm] * 5,
         out_specs=(vmem, vmem, vmem),
         scratch_shapes=scratch,
         compiler_params=pltpu.CompilerParams(
             collective_id=0, has_side_effects=True, vmem_limit_bytes=40 * 1024 * 1024
         ),
-    )(coherency, observed, flags, tile_map, jones)
+    )(*(pltpu.with_memory_space_constraint(x, pltpu.HBM) for x in (coherency, observed, flags, tile_map, jones)))
 
 
 def solution(mesh):

time: 50.8 us -> 44.4 us (0.87)
  local copies, waits for them, and re-layouts: 5.89 us -> 1.84 us
  Pallas kernels: 43.9 us -> 41.8 us
    unnamed x13 -> x3, local copies, waits for them, and re-layouts: 5.89 us -> 1.84 us
    pallas_call x1, Pallas kernels: 43.9 us -> 41.8 us  [body(): pl.pallas_call(kernel, out_shape=(jax.ShapeDtypeStruct((2, 12, 8, 32), F3...]
where the time goes in v2:
time: 44.4 us; the launch traced here: 44.2 us
  Pallas kernels  41.8 us (94%)
  local copies, waits for them, and re-layouts  1.84 us (4%)
  between operations  0.64 us (1%)
    pallas_call x1, Pallas kernels, body(): pl.pallas_call(kernel, out_shape=(jax.ShapeDtypeStruct((2, 12, 8, 32), F3...  41.8 us
    unnamed x3, local copies, waits for them, and re-layouts  1.84 us

profile of v2, /device:TPU:1, one launch (start us, length us, event | category | flops | bytes accessed | tf_op | source)
XLA Modules:
  0.0 44.2 jit_solution(11509768869093086962)
XLA Ops:
  0.6 41.8 %shard_map.76 = (f32[2,12,8,32]{3,2,1,0:T(8,128)S(1)}, f32[6,8,8]{2,1,0:T(8,128)S(1)}, f32[6,2,8]{2,1,0:T(2,128)S(1)}) custom-call(bf16[2,6,12,8,256]{4,3,2,1,0:T(8,128)(2,1)} %coherency.1, bf16[2,12,8,256]{3,2,1,0:T(8,128)(2,1)} %observed.1, s32[2,3]{1,0:T(2,128)} %flags_in.1, s32[2,2]{1,0:T(2,128)} %tile_map_in.1, f32[6,8,8]{2,1,0:T(8,128)} %jones_in.1), custom_call_target="tpu_custom_call" | custom-call | tf_op jit(solution)/shard_map/pallas_call | solution.py:445
  42.4 0.6 %copy.11 = f32[2,12,8,32]{3,2,1,0:T(8,128)} copy(f32[2,12,8,32]{3,2,1,0:T(8,128)S(1)} %get-tuple-element.6) | data formatting | bytes 49152
  43.0 0.6 %copy.12 = f32[6,8,8]{2,1,0:T(8,128)} copy(f32[6,8,8]{2,1,0:T(8,128)S(1)} %get-tuple-element.7) | data formatting | bytes 3072
  43.6 0.6 %copy.13 = f32[6,2,8]{2,1,0:T(2,128)} copy(f32[6,2,8]{2,1,0:T(2,128)S(1)} %get-tuple-element.8) | data formatting | bytes 768

commit v3 on v2

--- a/solution.py
+++ b/solution.py
@@ -101,9 +101,8 @@
     flags_in,
     tile_map_in,
     jones_in,
-    res_out,
-    grad_out,
-    curv_out,
+    stage,
+    owned,
     coh_raw,
     obs_raw,
     rows,
@@ -121,7 +120,6 @@
     pay,
     paid,
     jones_all,
-    stage,
     collect,
     flags,
     tile_map,
@@ -391,25 +389,37 @@
         wide = residual[half, c].reshape(24, 128)
         wide = pltpu.roll(wide, lax.rem(128 - 32 * part, 128), 1)
         stage[pl.ds(c, 24, stride=8), :] = wide
-    for t in range(2):
-        for s in range(12):
-            res_out[t, s] = stage[pl.ds(row_of(t, s) * 8, 8), 0:32]
 
     remote(paid, paid, send_sem.at[3], recv_sem.at[5], (tile, me)).wait_recv()
     terms = [pay[tile]] + [paid[number] for number in range(TILES - 1)]
     while len(terms) > 1:
         terms = [a + b for a, b in zip(terms[::2], terms[1::2])]
-    total = terms[0] * (1.0 / (12 * SB))
-    moved = [(pltpu.roll(total, 128 - 8 * g, 1) if g else total)[:, 0:8] for g in range(15)]
-    for k in range(6):
-        grad_out[k] = jnp.concatenate(moved[2 * k : 2 * k + 2], axis=0)
-        curv_out[k] = moved[12 + k // 2][k % 2 * 2 : k % 2 * 2 + 2]
+    owned[...] = terms[0] * (1.0 / (12 * SB))
 
     sent = jones_all.at[pl.ds(0, TILES - 1)]
     remote(sent, sent, send_sem.at[0], recv_sem.at[0], (tile, me)).wait_send()
     remote(taken, taken, send_sem.at[1], recv_sem.at[1], (tile, me)).wait_send()
     remote(taken, taken, send_sem.at[2], recv_sem.at[1], (tile, me)).wait_send()
     remote(paid, paid, send_sem.at[3], recv_sem.at[5], (tile, me)).wait_send()
+
+
+def unpack(stage, owned, res_out, grad_out, curv_out, res, grad, curv, sem):
+    total = owned[...]
+    moved = [(pltpu.roll(total, 128 - 8 * g, 1) if g else total)[:, 0:8] for g in range(15)]
+    for k in range(6):
+        grad[k] = jnp.concatenate(moved[2 * k : 2 * k + 2], axis=0)
+        curv[k] = moved[12 + k // 2][k % 2 * 2 : k % 2 * 2 + 2]
+    for t in range(2):
+        for s in range(12):
+            res[t, s] = stage[pl.ds(row_of(t, s) * 8, 8), 0:32]
+    copies = [
+        pltpu.make_async_copy(src, dst, sem.at[number])
+        for number, (src, dst) in enumerate(((res, res_out), (grad, grad_out), (curv, curv_out)))
+    ]
+    for copy in copies:
+        copy.start()
+    for copy in copies:
+        copy.wait()
 
 
 def body(coherency, observed, flags, tile_map, jones):
@@ -432,7 +442,6 @@
         pltpu.VMEM((TILES, 4, 128), F32),
         pltpu.VMEM((TILES - 1, 4, 128), F32),
         pltpu.VMEM((TILES, 4, 128), F32),
-        pltpu.VMEM((192, 128), F32),
         pltpu.VMEM((2, 256, 256), BF16),
         pltpu.SMEM((2, 3), jnp.int32),
         pltpu.SMEM((2, 2), jnp.int32),
@@ -442,20 +451,28 @@
         pltpu.SemaphoreType.DMA((6,)),
         pltpu.SemaphoreType.DMA((Z,)),
     ]
-    return pl.pallas_call(
+    summed = pl.pallas_call(
         kernel,
         out_shape=(
-            jax.ShapeDtypeStruct((2, 12, 8, 32), F32),
-            jax.ShapeDtypeStruct((6, 8, 8), F32),
-            jax.ShapeDtypeStruct((6, 2, 8), F32),
+            jax.ShapeDtypeStruct((192, 128), F32),
+            jax.ShapeDtypeStruct((4, 128), F32),
         ),
         in_specs=[hbm] * 5,
-        out_specs=(vmem, vmem, vmem),
+        out_specs=(vmem, vmem),
         scratch_shapes=scratch,
         compiler_params=pltpu.CompilerParams(
             collective_id=0, has_side_effects=True, vmem_limit_bytes=40 * 1024 * 1024
         ),
     )(*(pltpu.with_memory_space_constraint(x, pltpu.HBM) for x in (coherency, observed, flags, tile_map, jones)))
+    shapes = ((2, 12, 8, 32), (6, 8, 8), (6, 2, 8))
+    return pl.pallas_call(
+        unpack,
+        out_shape=tuple(jax.ShapeDtypeStruct(shape, F32) for shape in shapes),
+        in_specs=[vmem, vmem],
+        out_specs=(hbm, hbm, hbm),
+        scratch_shapes=[pltpu.VMEM(shape, F32) for shape in shapes] + [pltpu.SemaphoreType.DMA((3,))],
+        compiler_params=pltpu.CompilerParams(vmem_limit_bytes=8 * 1024 * 1024),
+    )(*summed)
 
 
 def solution(mesh):

time: 44.4 us -> 43.2 us (0.973)
  local copies, waits for them, and re-layouts: 1.84 us -> 0 us
  Pallas kernels: 41.8 us -> 42.4 us
    unnamed x3 -> x0, local copies, waits for them, and re-layouts: 1.84 us -> none
    pallas_call x1 -> x2, Pallas kernels: 41.8 us -> 42.4 us  [the longest x1 41.7 us: body(): pl.pallas_call(kernel, out_shape=(jax.ShapeDtypeStruct((192, 128), F32),...]
where the time goes in v3:
time: 43.2 us; the launch traced here: 43 us
  Pallas kernels  42.4 us (98%)
  between operations  0.64 us (1%)
    pallas_call x1, Pallas kernels, body(): pl.pallas_call(kernel, out_shape=(jax.ShapeDtypeStruct((192, 128), F32),...  41.7 us

profile of v3, /device:TPU:1, one launch (start us, length us, event | category | flops | bytes accessed | tf_op | source)
XLA Modules:
  0.0 43.0 jit_solution(2262739924159399677)
XLA Ops:
  0.6 41.7 %shard_map.76 = (f32[192,128]{1,0:T(8,128)S(1)}, f32[4,128]{1,0:T(4,128)S(1)}) custom-call(bf16[2,6,12,8,256]{4,3,2,1,0:T(8,128)(2,1)} %coherency.1, bf16[2,12,8,256]{3,2,1,0:T(8,128)(2,1)} %observed.1, s32[2,3]{1,0:T(2,128)} %flags_in.1, s32[2,2]{1,0:T(2,128)} %tile_map_in.1, f32[6,8,8]{2,1,0:T(8,128)} %jones_in.1), custom_call_target="tpu_custom_call" | custom-call | tf_op jit(solution)/shard_map/pallas_call | solution.py:454
  42.3 0.7 %shard_map.77 = (f32[2,12,8,32]{3,2,1,0:T(8,128)}, f32[6,8,8]{2,1,0:T(8,128)}, f32[6,2,8]{2,1,0:T(2,128)}) custom-call(f32[192,128]{1,0:T(8,128)S(1)} %get-tuple-element.5.stage, f32[4,128]{1,0:T(4,128)S(1)} %get-tuple-element.6.owned), custom_call_target="tpu_custom_call" | custom-call | tf_op jit(solution)/shard_map/pallas_call | solution.py:468

commit v4 on v3

--- a/solution.py
+++ b/solution.py
@@ -32,6 +32,7 @@
 )
 Z_NEAR_FIRST = (1, 7, 2, 6, 3, 5, 4)
 Z_FAR_FIRST = (4, 3, 5, 2, 6, 1, 7)
+DIR_FAR_FIRST = ((2, 1), (2, 0), (1, 1), (3, 1), (1, 0), (3, 0), (0, 1))
 YC_FAR_FIRST = ((2, 1), (2, 0), (1, 1), (3, 1), (1, 0), (3, 0), (0, 1))
 
 
@@ -121,6 +122,8 @@
     paid,
     jones_all,
     collect,
+    spread,
+    chosen_lane,
     flags,
     tile_map,
     jones,
@@ -139,6 +142,9 @@
             + lax.rem(core + dc, CORES)
         )
 
+    def along_dir(dx, dl):
+        return lax.rem(me // 2 + dx, DIRS // 2) * 2 + lax.rem(me + dl, 2)
+
     def remote(src, dst, send, recv, device):
         return pltpu.make_async_remote_copy(
             src_ref=src,
@@ -153,7 +159,7 @@
     greeted = (
         [(at(0, dz, 0), me) for dz in Z_FAR_FIRST]
         + [(at(dy, 0, dc), me) for dy, dc in YC_FAR_FIRST]
-        + [(tile, lax.rem(me + r, DIRS)) for r in range(1, DIRS)]
+        + [(tile, along_dir(dx, dl)) for dx, dl in DIR_FAR_FIRST]
     )
     for device in greeted:
         pl.semaphore_signal(barrier, inc=1, device_id=device, device_id_type=MESH)
@@ -221,6 +227,16 @@
                 both.append((jnp.maximum(upper, ahead) * kept).astype(F32))
             weight[h, g] = jnp.where(second, both[1], both[0])
 
+    row = lax.broadcasted_iota(jnp.int32, (6, 8, 256), 1)
+    direction = lax.broadcasted_iota(jnp.int32, (6, 8, 256), 0)
+    lane = lax.broadcasted_iota(jnp.int32, (6, 8, 256), 2)
+    chosen_lane[...] = jnp.where(lane % 128 // 8 == row // 4 * 8 + direction, 1.0, 0.0)
+    station = lax.broadcasted_iota(jnp.int32, (256, 256), 0)
+    station = station // 128 * 8 + station % 8
+    baseline = lax.broadcasted_iota(jnp.int32, (256, 256), 1)
+    for side in range(2):
+        takes = station == (baseline % SB if side else baseline // SB)
+        spread[side] = jnp.where(takes, 1.0, 0.0).astype(BF16)
     baseline = lax.broadcasted_iota(jnp.int32, (256, 256), 0)
     station = lax.broadcasted_iota(jnp.int32, (256, 256), 1)
     station = station // 128 * 8 + station % 8
@@ -239,26 +255,23 @@
     far = jones_all.at[pl.ds(0, count)]
     remote(far, far, send_sem.at[0], recv_sem.at[0], (at(1, 0, 0), me)).wait_recv()
 
-    row = lax.broadcasted_iota(jnp.int32, (6, 8, 256), 1)
-    direction = lax.broadcasted_iota(jnp.int32, (6, 8, 256), 0)
-    lane = lax.broadcasted_iota(jnp.int32, (6, 8, 256), 2)
-    own = lane % 128 // 8 == row // 4 * 8 + direction
-    station = lax.broadcasted_iota(jnp.int32, (256, 256), 0)
-    station = station // 128 * 8 + station % 8
-    baseline = lax.broadcasted_iota(jnp.int32, (256, 256), 1)
+    mask = chosen_lane[...]
     for side in range(2):
-        spread = jnp.where(station == (baseline % SB if side else baseline // SB), 1.0, 0.0)
-        spread = spread.astype(BF16)
+        picked = []
         for t in range(2):
             block = tile_map[t, side]
             both = jnp.concatenate([jones_all[2 * block], jones_all[2 * block + 1]], axis=1)
             both = jnp.concatenate([both, both], axis=0)
-            chosen = jnp.where(own, both[None], 0.0).reshape(48, 256)
-            high, low = split(chosen)
-            full = jnp.dot(high, spread, preferred_element_type=F32)
-            full = full + jnp.dot(low, spread, preferred_element_type=F32)
+            picked.append(jnp.where(mask != 0.0, both[None], 0.0).reshape(48, 256))
+        high, low = split(jnp.concatenate(picked, axis=0))
+        full = jnp.dot(
+            jnp.concatenate([high, low], axis=0), spread[side], preferred_element_type=F32
+        )
+        full = full[0:96] + full[96:192]
+        for t in range(2):
             for h in range(2):
-                gains[side, t, h] = full[:, h * 128 : h * 128 + 128].reshape(6, 8, 128)
+                block = full[t * 48 : t * 48 + 48, h * 128 : h * 128 + 128]
+                gains[side, t, h] = block.reshape(6, 8, 128)
 
     def gain(side, k, h):
         return [
@@ -288,11 +301,11 @@
             for c in range(8):
                 partial[c, h, g] = total[g * 8 + c]
 
-        for r in range(1, DIRS):
-            other = lax.rem(me + r, DIRS)
+        for number, (dx, dl) in enumerate(DIR_FAR_FIRST):
+            other = along_dir(dx, dl)
             remote(
                 partial.at[other, h],
-                taken.at[h, r - 1],
+                taken.at[h, number],
                 send_sem.at[1],
                 recv_sem.at[1 + h],
                 (tile, other),
@@ -332,8 +345,8 @@
         seen = obs_rows[h, pl.ds(me, 24, stride=8), :].reshape(3, 8, 128)
         residual[h, me] = weight[h] * (seen - model)
         done = residual.at[h, me]
-        for r in range(1, DIRS):
-            other = lax.rem(me + r, DIRS)
+        for dx, dl in DIR_FAR_FIRST:
+            other = along_dir(dx, dl)
             remote(done, done, send_sem.at[2], recv_sem.at[3 + h], (tile, other)).start()
 
     for h in range(2):
@@ -359,9 +372,10 @@
     parts = []
     for side, val in ((0, val_p), (1, val_q)):
         high, low = split(val[...].reshape(128, 256))
-        sums = jnp.dot(high, collect[side], preferred_element_type=F32)
-        sums = sums + jnp.dot(low, collect[side], preferred_element_type=F32)
-        sums = sums.reshape(16, 8, 256)
+        sums = jnp.dot(
+            jnp.concatenate([high, low], axis=0), collect[side], preferred_element_type=F32
+        )
+        sums = (sums[0:128] + sums[128:256]).reshape(16, 8, 256)
         halves = []
         for h in range(2):
             piece = jnp.zeros((8, 128), F32)
@@ -443,6 +457,8 @@
         pltpu.VMEM((TILES - 1, 4, 128), F32),
         pltpu.VMEM((TILES, 4, 128), F32),
         pltpu.VMEM((2, 256, 256), BF16),
+        pltpu.VMEM((2, 256, 256), BF16),
+        pltpu.VMEM((6, 8, 256), F32),
         pltpu.SMEM((2, 3), jnp.int32),
         pltpu.SMEM((2, 2), jnp.int32),
         pltpu.VMEM((6, 8, 8), F32),

time: 43.2 us -> 42.8 us (level)
  no operation moved by 1% of the time
where the time goes in v4:
time: 42.8 us; the launch traced here: 42.7 us
  Pallas kernels  42 us (98%)
  between operations  0.64 us (1%)
    pallas_call x1, Pallas kernels, body(): pl.pallas_call(kernel, out_shape=(jax.ShapeDtypeStruct((192, 128), F32),...  41.3 us

profile of v4, /device:TPU:1, one launch (start us, length us, event | category | flops | bytes accessed | tf_op | source)
XLA Modules:
  0.0 42.7 jit_solution(7596049173214760144)
XLA Ops:
  0.6 41.3 %shard_map.76 = (f32[192,128]{1,0:T(8,128)S(1)}, f32[4,128]{1,0:T(4,128)S(1)}) custom-call(bf16[2,6,12,8,256]{4,3,2,1,0:T(8,128)(2,1)} %coherency.1, bf16[2,12,8,256]{3,2,1,0:T(8,128)(2,1)} %observed.1, s32[2,3]{1,0:T(2,128)} %flags_in.1, s32[2,2]{1,0:T(2,128)} %tile_map_in.1, f32[6,8,8]{2,1,0:T(8,128)} %jones_in.1), custom_call_target="tpu_custom_call" | custom-call | tf_op jit(solution)/shard_map/pallas_call | solution.py:470
  42.0 0.7 %shard_map.77 = (f32[2,12,8,32]{3,2,1,0:T(8,128)}, f32[6,8,8]{2,1,0:T(8,128)}, f32[6,2,8]{2,1,0:T(2,128)}) custom-call(f32[192,128]{1,0:T(8,128)S(1)} %get-tuple-element.5.stage, f32[4,128]{1,0:T(4,128)S(1)} %get-tuple-element.6.owned), custom_call_target="tpu_custom_call" | custom-call | tf_op jit(solution)/shard_map/pallas_call | solution.py:484

commit v5 on v4

--- a/solution.py
+++ b/solution.py
@@ -180,12 +180,17 @@
         copy.start()
 
     here[0].wait()
-    packed = jnp.zeros((8, 128), F32)
-    for k in range(6):
-        wide = jnp.concatenate([jones[k], jnp.zeros((8, 120), F32)], axis=1)
-        packed = packed + (pltpu.roll(wide, 8 * k, 1) if k else wide)
-    packed = packed[0:4] + pltpu.roll(packed, 64, 1)[4:8]
-    jones_all[tile] = packed
+    mine_at = lax.broadcasted_iota(jnp.int32, (8, 128), 1) // 8
+    component = lax.broadcasted_iota(jnp.int32, (8, 128), 0)
+    for pair in range(3):
+        packed = jnp.zeros((8, 128), F32)
+        for k in range(2):
+            wide = jnp.concatenate([jones[2 * pair + k], jnp.zeros((8, 120), F32)], axis=1)
+            for shift in (8, 16, 32):
+                wide = wide + pltpu.roll(wide, shift, 1)
+            wide = pltpu.roll(wide, 64, 1) if k else wide
+            packed = jnp.where(mine_at == 8 * k + component, wide, packed)
+        jones_all[tile, pair : pair + 1] = jnp.sum(packed, axis=0, keepdims=True)
 
     pl.semaphore_wait(barrier, len(greeted))
 
@@ -227,10 +232,9 @@
                 both.append((jnp.maximum(upper, ahead) * kept).astype(F32))
             weight[h, g] = jnp.where(second, both[1], both[0])
 
-    row = lax.broadcasted_iota(jnp.int32, (6, 8, 256), 1)
-    direction = lax.broadcasted_iota(jnp.int32, (6, 8, 256), 0)
-    lane = lax.broadcasted_iota(jnp.int32, (6, 8, 256), 2)
-    chosen_lane[...] = jnp.where(lane % 128 // 8 == row // 4 * 8 + direction, 1.0, 0.0)
+    row = lax.broadcasted_iota(jnp.int32, (48, 256), 0)
+    lane = lax.broadcasted_iota(jnp.int32, (48, 256), 1)
+    chosen_lane[...] = jnp.where(lane % 128 // 8 == row % 16, 1.0, 0.0)
     station = lax.broadcasted_iota(jnp.int32, (256, 256), 0)
     station = station // 128 * 8 + station % 8
     baseline = lax.broadcasted_iota(jnp.int32, (256, 256), 1)
@@ -261,8 +265,8 @@
         for t in range(2):
             block = tile_map[t, side]
             both = jnp.concatenate([jones_all[2 * block], jones_all[2 * block + 1]], axis=1)
-            both = jnp.concatenate([both, both], axis=0)
-            picked.append(jnp.where(mask != 0.0, both[None], 0.0).reshape(48, 256))
+            rows_of = [jnp.broadcast_to(both[pair : pair + 1], (16, 256)) for pair in range(3)]
+            picked.append(jnp.where(mask != 0.0, jnp.concatenate(rows_of, axis=0), 0.0))
         high, low = split(jnp.concatenate(picked, axis=0))
         full = jnp.dot(
             jnp.concatenate([high, low], axis=0), spread[side], preferred_element_type=F32
@@ -296,7 +300,7 @@
                 out += [total[g * 8 + c] + v[c] for c in range(8)]
             return tuple(out)
 
-        total = lax.fori_loop(0, 6, add_direction, (jnp.zeros((8, 128), F32),) * 24)
+        total = lax.fori_loop(0, 6, add_direction, (jnp.zeros((8, 128), F32),) * 24, unroll=2)
         for g in range(3):
             for c in range(8):
                 partial[c, h, g] = total[g * 8 + c]
@@ -455,10 +459,10 @@
         pltpu.VMEM((16, 8, 256), F32),
         pltpu.VMEM((TILES, 4, 128), F32),
         pltpu.VMEM((TILES - 1, 4, 128), F32),
-        pltpu.VMEM((TILES, 4, 128), F32),
+        pltpu.VMEM((TILES, 3, 128), F32),
         pltpu.VMEM((2, 256, 256), BF16),
         pltpu.VMEM((2, 256, 256), BF16),
-        pltpu.VMEM((6, 8, 256), F32),
+        pltpu.VMEM((48, 256), F32),
         pltpu.SMEM((2, 3), jnp.int32),
         pltpu.SMEM((2, 2), jnp.int32),
         pltpu.VMEM((6, 8, 8), F32),

time: 42.8 us -> 42.7 us (level)
  no operation moved by 1% of the time
where the time goes in v5:
time: 42.7 us; the launch traced here: 42.5 us
  Pallas kernels  41.9 us (98%)
  between operations  0.64 us (1%)
    pallas_call x1, Pallas kernels, body(): pl.pallas_call(kernel, out_shape=(jax.ShapeDtypeStruct((192, 128), F32),...  41.2 us

profile of v5, /device:TPU:1, one launch (start us, length us, event | category | flops | bytes accessed | tf_op | source)
XLA Modules:
  0.0 42.5 jit_solution(7474871729736466971)
XLA Ops:
  0.6 41.2 %shard_map.76 = (f32[192,128]{1,0:T(8,128)S(1)}, f32[4,128]{1,0:T(4,128)S(1)}) custom-call(bf16[2,6,12,8,256]{4,3,2,1,0:T(8,128)(2,1)} %coherency.1, bf16[2,12,8,256]{3,2,1,0:T(8,128)(2,1)} %observed.1, s32[2,3]{1,0:T(2,128)} %flags_in.1, s32[2,2]{1,0:T(2,128)} %tile_map_in.1, f32[6,8,8]{2,1,0:T(8,128)} %jones_in.1), custom_call_target="tpu_custom_call" | custom-call | tf_op jit(solution)/shard_map/pallas_call | solution.py:474
  41.8 0.7 %shard_map.77 = (f32[2,12,8,32]{3,2,1,0:T(8,128)}, f32[6,8,8]{2,1,0:T(8,128)}, f32[6,2,8]{2,1,0:T(2,128)}) custom-call(f32[192,128]{1,0:T(8,128)S(1)} %get-tuple-element.5.stage, f32[4,128]{1,0:T(4,128)S(1)} %get-tuple-element.6.owned), custom_call_target="tpu_custom_call" | custom-call | tf_op jit(solution)/shard_map/pallas_call | solution.py:488

commit v6 on v5

--- a/solution.py
+++ b/solution.py
@@ -370,7 +370,7 @@
                 val_q[2 * k + j, :, h * 128 : h * 128 + 128] = fold(b[4 * j : 4 * j + 4])
             return carry
 
-        lax.fori_loop(0, 6, one_direction, 0)
+        lax.fori_loop(0, 6, one_direction, 0, unroll=3)
 
     group = lax.broadcasted_iota(jnp.int32, (8, 128), 1) // 8
     parts = []

time: 42.7 us -> 42.6 us (level)
  no operation moved by 1% of the time
where the time goes in v6:
time: 42.6 us; the launch traced here: 42.5 us
  Pallas kernels  41.9 us (98%)
  between operations  0.64 us (2%)
    pallas_call x1, Pallas kernels, body(): pl.pallas_call(kernel, out_shape=(jax.ShapeDtypeStruct((192, 128), F32),...  41.1 us

profile of v6, /device:TPU:1, one launch (start us, length us, event | category | flops | bytes accessed | tf_op | source)
XLA Modules:
  0.0 42.5 jit_solution(14399760292438796076)
XLA Ops:
  0.6 41.1 %shard_map.76 = (f32[192,128]{1,0:T(8,128)S(1)}, f32[4,128]{1,0:T(4,128)S(1)}) custom-call(bf16[2,6,12,8,256]{4,3,2,1,0:T(8,128)(2,1)} %coherency.1, bf16[2,12,8,256]{3,2,1,0:T(8,128)(2,1)} %observed.1, s32[2,3]{1,0:T(2,128)} %flags_in.1, s32[2,2]{1,0:T(2,128)} %tile_map_in.1, f32[6,8,8]{2,1,0:T(8,128)} %jones_in.1), custom_call_target="tpu_custom_call" | custom-call | tf_op jit(solution)/shard_map/pallas_call | solution.py:474
  41.8 0.7 %shard_map.77 = (f32[2,12,8,32]{3,2,1,0:T(8,128)}, f32[6,8,8]{2,1,0:T(8,128)}, f32[6,2,8]{2,1,0:T(2,128)}) custom-call(f32[192,128]{1,0:T(8,128)S(1)} %get-tuple-element.5.stage, f32[4,128]{1,0:T(4,128)S(1)} %get-tuple-element.6.owned), custom_call_target="tpu_custom_call" | custom-call | tf_op jit(solution)/shard_map/pallas_call | solution.py:488

commit v7 on v5

--- a/solution.py
+++ b/solution.py
@@ -389,18 +389,20 @@
         parts.append((side, 0, jnp.where(second, pltpu.roll(halves[1], 4, 0), halves[0])))
         parts.append((side, 1, jnp.where(second, halves[1], pltpu.roll(halves[0], 4, 0))))
 
-    for b in range(TILES // 2):
+    number = 0
+    for dy, dz in dict.fromkeys(offset[:2] for offset in FAR_FIRST):
+        b = lax.rem(y + dy, YH) * Z + lax.rem(z + dz, Z)
         block = jnp.zeros((8, 128), F32)
         for side, t, part in parts:
             block = block + jnp.where(tile_map[t, side] == b, part, 0.0)
         pay[2 * b] = block[0:4]
         pay[2 * b + 1] = block[4:8]
-
-    for number, (dy, dz, dc) in enumerate(FAR_FIRST):
-        owner = at(dy, dz, dc)
-        remote(
-            pay.at[owner], paid.at[number], send_sem.at[3], recv_sem.at[5], (owner, me)
-        ).start()
+        for dc in (1, 0) if dy or dz else (1,):
+            owner = at(dy, dz, dc)
+            remote(
+                pay.at[owner], paid.at[number], send_sem.at[3], recv_sem.at[5], (owner, me)
+            ).start()
+            number += 1
 
     half, part = me // 4, me % 4
     for c in range(8):

time: 42.7 us -> 42.6 us (level)
  no operation moved by 1% of the time
where the time goes in v7:
time: 42.6 us; the launch traced here: 42.5 us
  Pallas kernels  41.8 us (98%)
  between operations  0.64 us (2%)
    pallas_call x1, Pallas kernels, body(): pl.pallas_call(kernel, out_shape=(jax.ShapeDtypeStruct((192, 128), F32),...  41.1 us

profile of v7, /device:TPU:1, one launch (start us, length us, event | category | flops | bytes accessed | tf_op | source)
XLA Modules:
  0.0 42.5 jit_solution(2542582647799621535)
XLA Ops:
  0.6 41.1 %shard_map.76 = (f32[192,128]{1,0:T(8,128)S(1)}, f32[4,128]{1,0:T(4,128)S(1)}) custom-call(bf16[2,6,12,8,256]{4,3,2,1,0:T(8,128)(2,1)} %coherency.1, bf16[2,12,8,256]{3,2,1,0:T(8,128)(2,1)} %observed.1, s32[2,3]{1,0:T(2,128)} %flags_in.1, s32[2,2]{1,0:T(2,128)} %tile_map_in.1, f32[6,8,8]{2,1,0:T(8,128)} %jones_in.1), custom_call_target="tpu_custom_call" | custom-call | tf_op jit(solution)/shard_map/pallas_call | solution.py:476
  41.7 0.7 %shard_map.77 = (f32[2,12,8,32]{3,2,1,0:T(8,128)}, f32[6,8,8]{2,1,0:T(8,128)}, f32[6,2,8]{2,1,0:T(2,128)}) custom-call(f32[192,128]{1,0:T(8,128)S(1)} %get-tuple-element.5.stage, f32[4,128]{1,0:T(4,128)S(1)} %get-tuple-element.6.owned), custom_call_target="tpu_custom_call" | custom-call | tf_op jit(solution)/shard_map/pallas_call | solution.py:490
